TPU v7x, 32 devices: a whole 2x2x4 slice. The times are simulated.
32 devices in a mesh: groups: 2 (over x), tm: 4 (over y, core), ingest: 4 (over z).
Axes of the slice: x: 2, y: 2, z: 4, core: 2. Of those that a mesh axis runs over, the one named last changes fastest.
Arguments:
- transition: float32 [512, 512], replicated, may hold values from -1.01 to 1.01
- gain: float32 [512, 512], replicated, may hold values from -0.01 to 0.21
- smoother_gain: float32 [512, 512], replicated, may hold values from -1.01 to 1.01
- start_state: float32 [1024], P('groups'), parts along dimension 0, may hold values from -6 to 6
- rows_float: float32 [6, 2, 32, 16], P(None, None, ('groups', 'tm', 'ingest')), parts along dimension 2, may hold values from -6 to 6, as said below
- rows_index: int32 [2, 2, 32, 16], P(None, None, ('groups', 'tm', 'ingest')), parts along dimension 2, may hold values from 0 to 127, as said below
Outputs:
- filtered: float32 [128, 512], P(('groups', 'tm', 'ingest')), parts along dimension 0
- smoothed: float32 [128, 512], P(('groups', 'tm', 'ingest')), parts along dimension 0
There are 2 independent parts, one for each index of `groups`. A program takes and returns all parts, laid end to end along the dimension named above; an argument that names none is the same for every part. Nothing has to cross between parts.
Inputs may be any that keep to these rules, and one draw needn't show every extreme that they name: rows_index[0] is a step within the owner, or 4 for an empty slot; rows_index[1] is a state block below 128. rows_float[0] readings; rows_float[1] precisions between 0.5 and 2; rows_float[2] to rows_float[5] coefficients within -0.7 to 0.7.
All inputs are finite; a program needn't handle non-finite values.
Results may differ from a plain program's by a relative error of at most 0.0003.
Values sent between devices are 32-bit elements; how exact they have to be, the bound alone decides.
A program may use at most 128 MiB of HBM per device.

v0:
```python
import jax
import jax.numpy as jnp
from jax import lax
from jax.sharding import PartitionSpec as P

STEPS_DEV = 4


highest = lax.Precision.HIGHEST


def entering(value, axis, join, neutral, backward):
    count, mine = (lax.axis_size(axis), lax.axis_index(axis))
    pieces = jax.tree.map(lambda part: lax.all_gather(part, axis), value)
    if backward:
        pieces = jax.tree.map(lambda part: part[::-1], pieces)
        mine = count - 1 - mine
    total = jax.tree.map(
        lambda part, zero: jnp.full_like(part, 0) + jnp.asarray(zero, part.dtype), value, neutral
    )

    def turn(position, total):
        longer = join(total, jax.tree.map(lambda part: part[position], pieces))
        return jax.tree.map(lambda new, old: jnp.where(position < mine, new, old), longer, total)

    return lax.fori_loop(0, count - 1, turn, total)


def from_root(shard, axis, root):
    mine = lax.axis_index(axis) == root
    return lax.psum(jnp.where(mine, shard, jnp.zeros_like(shard)), axis)


def product(matrix_a, matrix_b):
    return jnp.dot(matrix_a, matrix_b, precision=highest, preferred_element_type=jnp.float32)


def chain_link(earlier, later):
    return (product(later[0], earlier[0]), product(later[0], earlier[1]) + later[1])


def on_device(transition, gain, smoother_gain, start_state, rows_float, rows_index):
    received_float = lax.all_to_all(
        rows_float, ("tm", "ingest"), split_axis=3, concat_axis=2, tiled=True
    )
    received_index = lax.all_to_all(
        rows_index, ("tm", "ingest"), split_axis=3, concat_axis=2, tiled=True
    )
    states = transition.shape[0]
    blocks = states // 4
    values = received_float.reshape(6, -1)
    indices = received_index.reshape(2, -1)
    slot_total = values.shape[1]
    readings = values[0]
    precisions = values[1]
    coefficients = values[2:]
    onehot = (indices[1][:, None] == jnp.arange(blocks, dtype=jnp.int32)[None, :]).astype(
        jnp.float32
    )
    design = (onehot[:, :, None] * jnp.transpose(coefficients)[:, None, :]).reshape(
        slot_total, states
    )
    design_next = product(design, transition)
    spread = product(gain, jnp.transpose(design))
    step_ids = jnp.arange(STEPS_DEV, dtype=jnp.int32)
    select = (indices[0][None, :] == step_ids[:, None]).astype(jnp.float32) * precisions[None, :]
    inflow = product(select * readings[None, :], jnp.transpose(spread))
    identity = jnp.eye(states, dtype=jnp.float32)
    empty_vector = jnp.zeros((states,), jnp.float32)
    inner_count = lax.axis_size("ingest")

    def element_step(element, inputs):
        select_row, inflow_row = inputs
        step_matrix = transition - product(spread * select_row[None, :], design_next)
        return (
            (product(step_matrix, element[0]), product(step_matrix, element[1]) + inflow_row),
            None,
        )

    (block_map, block_offset), _ = lax.scan(
        element_step, (identity, empty_vector), (select, inflow)
    )
    inner_before = entering(
        (block_map, block_offset), "ingest", chain_link, (identity, empty_vector), False
    )
    inner_through = chain_link(inner_before, (block_map, block_offset))
    group_map, group_offset = (
        from_root(inner_through[0], "ingest", inner_count - 1),
        from_root(inner_through[1], "ingest", inner_count - 1),
    )
    outer_before = entering(
        (group_map, group_offset), "tm", chain_link, (identity, empty_vector), False
    )
    before_map, before_offset = chain_link(outer_before, inner_before)
    state_entry = product(before_map, start_state) + before_offset

    def filter_step(previous, inputs):
        select_row, inflow_row = inputs
        updated = (
            product(transition, previous)
            - product(spread, select_row * product(design_next, previous))
            + inflow_row
        )
        return (updated, updated)

    _, filtered = lax.scan(filter_step, state_entry, (select, inflow))
    position = lax.axis_index(("tm", "ingest"))
    device_count = lax.axis_size(("tm", "ingest"))
    pushed = product(product(filtered, jnp.transpose(transition)), jnp.transpose(smoother_gain))
    final_row = (position == device_count - 1) & (step_ids == STEPS_DEV - 1)
    residue = filtered - jnp.where(final_row[:, None], 0.0, pushed)

    def tail_step(running, residue_row):
        return (product(smoother_gain, running) + residue_row, None)

    tail_offset, _ = lax.scan(tail_step, empty_vector, residue, reverse=True)
    gain_power = lax.fori_loop(
        0, STEPS_DEV - 1, lambda turn, current: product(smoother_gain, current), smoother_gain
    )
    later_inner = entering(
        (gain_power, tail_offset), "ingest", chain_link, (identity, empty_vector), True
    )
    later_through = chain_link(later_inner, (gain_power, tail_offset))
    later_group = (
        from_root(later_through[0], "ingest", 0),
        from_root(later_through[1], "ingest", 0),
    )
    later_outer = entering(later_group, "tm", chain_link, (identity, empty_vector), True)
    _, smooth_entry = chain_link(later_outer, later_inner)

    def smooth_step(following, residue_row):
        current = product(smoother_gain, following) + residue_row
        return (current, current)

    _, smoothed = lax.scan(smooth_step, smooth_entry, residue, reverse=True)
    return (filtered, smoothed)


def solution(mesh):
    placed = (
        P(),
        P(),
        P(),
        P("groups"),
        P(None, None, ("groups", "tm", "ingest"), None),
        P(None, None, ("groups", "tm", "ingest"), None),
    )
    return jax.shard_map(
        on_device,
        mesh=mesh,
        in_specs=placed,
        out_specs=(P(("groups", "tm", "ingest"), None), P(("groups", "tm", "ingest"), None)),
        check_vma=False,
    )
```

profile of v0, /device:TPU:0, one launch (start us, length us, event | category | flops | bytes accessed | tf_op | source)
XLA Modules:
  0.0 529.8 jit_solution(12607902924485451307)
XLA Ops:
  8.7 7.4 %all-to-all-start = ((s32[2,2,1,16]{1,0,2,3:T(2,128)}), s32[2,2,1,16]{1,0,2,3:T(2,128)S(1)}, u32[]{:S(2)}, u32[]{:S(2)}) async-start(s32[2,2,1,16]{1,0,2,3:T(2,128)} %copy.22), calls=%async_computation | async-start | bytes 32768 | tf_op jit(solution)/shard_map/all_to_all | solution.py:46
  18.7 3.8 all-to-all-done
  22.5 3.5 all-to-all-start.1
  26.4 6.0 %all-to-all-done.1 = f32[6,2,1,16]{0,1,2,3:T(2,128)S(1)} async-done(((f32[6,2,1,16]{0,1,2,3:T(2,128)}), f32[6,2,1,16]{0,1,2,3:T(2,128)S(1)}, u32[]{:S(2)}, u32[]{:S(2)}) %all-to-all-start.1) | async-done | bytes 800 | tf_op jit(solution)/shard_map/all_to_all | solution.py:43
  38.6 24.4 %while.131 = (s32[]{:T(128)}, f32[512,512]{1,0:T(8,128)}, f32[512]{0:T(512)S(1)}, f32[4,32]{1,0:T(4,128)S(1)}, f32[512,32]{1,0:T(8,128)S(1)}, /*index=5*/f32[32,...) while((s32[]{:T(128)}, f32[512,512]{1,0:T(8,128)}, ...), condition=%wide.region_1.2_spmd.clone, body=%wide.region_0.1_spmd.clone.sunk | while | flops 1714701312 | bytes 8538623 | solution.py:80
  40.9 2.9 fusion.171
  47.0 2.9 fusion.171
  53.1 2.9 fusion.171
  59.2 2.9 fusion.171
  65.4 12.1 %all-gather.4 = f32[4,1,512]{2,1,0:T(1,128)S(1)} all-gather(f32[1,1,512]{2,1,0:T(1,128)S(1)} %bitcast.316), channel_id=3, replica_groups=mesh['groups'=2,'tm'=4,'ingest'=4] {'ingest'}, dimensions={0}, use_global_device_ids=true | all-gather | bytes 10240 | tf_op jit(solution)/shard_map/all_gather | solution.py:14
  77.5 63.9 %all-gather.17.cloned.1.call-done = f32[2048,512]{1,0:T(8,128)} async-done(((f32[512,512]{1,0:T(8,128)}), f32[2048,512]{1,0:T(8,128)}) %all-gather.17.cloned.1.call-update) | async-done | bytes 4194320 | tf_op jit(solution)/shard_map/all_gather | solution.py:14
  141.4 22.6 %while.132 = (s32[]{:T(128)}, f32[512,512]{1,0:T(8,128)}, f32[512]{0:T(512)S(1)}, s32[]{:T(128)}, f32[4,512,512]{2,1,0:T(8,128)}, /*index=5*/f32[4,512]{1,0:T(4,128)S(1)}, s32[]{:T(128)}, s32[]{:T(128)}) while((s32[]{:T(128)}, f32[512,512]{1,0:T(8,128)}, f32[512]{0:T(512)S(1)}, s32[]{:T(128)}, f32[4,512,512]{2,1,0:T(8,128)}, ...), condition=%wide.region_3.4_spmd.clone, body=%wide.region_2.3_spmd.clone.sunk | while | flops 1614022656 | bytes 7360639 | solution.py:26
  142.6 4.0 convolution_select_fusion.9
  150.2 4.0 convolution_select_fusion.9
  157.7 4.0 convolution_select_fusion.9
  164.0 4.4 fusion.30
  169.7 12.1 %while.129 = (s32[]{:T(128)}, f32[512,512]{1,0:T(8,128)}, f32[512,512]{1,0:T(8,128)S(1)}, s32[]{:T(128)}) while((s32[]{:T(128)}, f32[512,512]{1,0:T(8,128)}, f32[512,512]{1,0:T(8,128)S(1)}, s32[]{:T(128)}) %tuple.271), condition=%wide.region_11.12_spmd, body=%wide.region_10.11_spmd.sunk | while | flops 1610612736 | bytes 5242933 | solution.py:117
  170.9 2.8 fusion.161
  175.0 2.8 fusion.161
  179.0 2.8 fusion.161
  181.9 37.1 %all-reduce.3.cloned.1.call-done = f32[1,512,512]{2,1,0:T(8,128)} async-done(((f32[1,512,512]{2,1,0:T(8,128)}), f32[1,512,512]{2,1,0:T(8,128)}) %all-reduce.3.cloned.1.call-update) | async-done | bytes 1048592 | tf_op jit(solution)/shard_map/psum | solution.py:31
  221.3 79.5 %all-gather.19.cloned.1.call-done = f32[2048,512]{1,0:T(8,128)} async-done(((f32[512,512]{1,0:T(8,128)}), f32[2048,512]{1,0:T(8,128)}) %all-gather.19.cloned.1.call-update) | async-done | bytes 4194320 | tf_op jit(solution)/shard_map/all_gather | solution.py:14
  300.8 4.6 rev.12
  307.7 8.9 %psum.29 = f32[1,512]{1,0:T(1,128)S(1)} all-reduce(f32[1,512]{1,0:T(1,128)S(1)} %bitcast.329), channel_id=1, replica_groups=mesh['groups'=2,'tm'=4,'ingest'=4] {'ingest'}, use_global_device_ids=true, to_apply=%region_5.6 | all-reduce | flops 512 | bytes 4096 | tf_op jit(solution)/shard_map/psum | solution.py:31
  316.6 5.2 all-gather.5
  321.8 13.6 %all-gather.13.cloned.1.call-done = f32[4,512,512]{2,1,0:T(8,128)} async-done(((f32[1,512,512]{2,1,0:T(8,128)}), f32[4,512,512]{2,1,0:T(8,128)}) %all-gather.13.cloned.1.call-update) | async-done | bytes 4194320 | tf_op jit(solution)/shard_map/all_gather | solution.py:14
  335.4 27.7 %while.133 = (s32[]{:T(128)}, f32[512,512]{1,0:T(8,128)}, f32[512]{0:T(512)S(1)}, s32[]{:T(128)}, f32[4,512,512]{2,1,0:T(8,128)}, /*index=5*/f32[4,512]{1,0:T(4,128)S(1)}, s32[]{:T(128)}, s32[]{:T(128)}) while((s32[]{:T(128)}, f32[512,512]{1,0:T(8,128)}, f32[512]{0:T(512)S(1)}, s32[]{:T(128)}, f32[4,512,512]{2,1,0:T(8,128)}, ...), condition=%wide.region_7.8_spmd.clone, body=%wide.region_6.7_spmd.clone.sunk | while | flops 1614022656 | bytes 7360639 | solution.py:26
  337.7 4.7 convolution_select_fusion.10
  344.6 2.3 copy.127
  346.9 4.7 convolution_select_fusion.10
  353.9 2.3 copy.127
  356.1 4.7 convolution_select_fusion.10
  363.1 3.4 fusion.51
  369.7 6.3 %while.128 = (s32[]{:T(128)}, f32[512]{0:T(512)S(1)}, f32[4,512]{1,0:T(4,128)S(1)}, f32[512,512]{1,0:T(8,128)S(1)}, f32[4,32]{1,0:T(4,128)S(1)}, /*index=5*/f32[...) while((s32[]{:T(128)}, f32[512]{0:T(512)S(1)}, ...), condition=%wide.region_9.10_spmd, body=%wide.region_8.9_spmd.sunk | while | flops 3540002 | bytes 1204729 | solution.py:106
  377.9 4.2 while.134
  382.1 12.1 %all-gather.6 = f32[4,1,512]{2,1,0:T(1,128)S(1)} all-gather(f32[1,1,512]{2,1,0:T(1,128)S(1)} %bitcast.315), channel_id=5, replica_groups=mesh['groups'=2,'tm'=4,'ingest'=4] {'ingest'}, dimensions={0}, use_global_device_ids=true | all-gather | bytes 10240 | tf_op jit(solution)/shard_map/all_gather | solution.py:14
  394.4 21.0 %while.135 = (s32[]{:T(128)}, f32[512,512]{1,0:T(8,128)S(1)}, f32[512]{0:T(512)S(1)}, s32[]{:T(128)}, f32[4,512,512]{2,1,0:T(8,128)}, /*index=5*/f32[4,512]{1,0:T(4,128)S(1)}, s32[]{:T(128)}, s32[]{:T(128)}) while((s32[]{:T(128)}, f32[512,512]{1,0:T(8,128)S(1)}, f32[512]{0:T(512)S(1)}, s32[]{:T(128)}, ...), condition=%wide.region_15.16_spmd.clone, body=%wide.region_14.15_spmd.clone.sunk | while | flops 1614022656 | bytes 7360639 | solution.py:26
  395.4 3.7 convolution_select_fusion.11
  402.4 3.7 convolution_select_fusion.11
  409.4 3.7 convolution_select_fusion.11
  415.4 4.0 fusion.29
  419.5 50.6 %all-reduce.5.cloned.1.call-done = f32[1,512,512]{2,1,0:T(8,128)} async-done(((f32[1,512,512]{2,1,0:T(8,128)}), f32[1,512,512]{2,1,0:T(8,128)}) %all-reduce.5.cloned.1.call-update) | async-done | bytes 1048592 | tf_op jit(solution)/shard_map/psum | solution.py:31
  472.4 10.2 %psum.31 = f32[1,512]{1,0:T(1,128)S(1)} all-reduce(f32[1,512]{1,0:T(1,128)S(1)} %bitcast.330), channel_id=1, replica_groups=mesh['groups'=2,'tm'=4,'ingest'=4] {'ingest'}, use_global_device_ids=true, to_apply=%region_17.18 | all-reduce | flops 512 | bytes 4096 | tf_op jit(solution)/shard_map/psum | solution.py:31
  482.6 5.2 all-gather.7
  487.9 17.7 %all-gather.15.cloned.1.call-done = f32[4,512,512]{2,1,0:T(8,128)} async-done(((f32[1,512,512]{2,1,0:T(8,128)}), f32[4,512,512]{2,1,0:T(8,128)}) %all-gather.15.cloned.1.call-update) | async-done | bytes 4194320 | tf_op jit(solution)/shard_map/all_gather | solution.py:14
  505.6 4.6 rev.14
  510.2 6.8 %while.136 = (s32[]{:T(128)}, f32[512]{0:T(512)S(1)}, s32[]{:T(128)}, f32[4,512,512]{2,1,0:T(8,128)}, f32[4,512]{1,0:T(4,128)S(1)}, /*index=5*/s32[]{:T(128)}, s32[]{:T(128)}) while((s32[]{:T(128)}, f32[512]{0:T(512)S(1)}, s32[]{:T(128)}, f32[4,512,512]{2,1,0:T(8,128)}, f32[4,512]{1,0:T(4,128)S(1)}, /*index=5*/s32[]{:T(128)}, ...), condition=%wide.region_19.20_spmd.clone, body=%wide.region_18.19_spmd.clone.sunk | while | flops 3147780 | bytes 1069170 | solution.py:26
  518.0 4.4 while.130
  (229 shorter events, 94.9 us)
Async XLA Ops:
  7.2 26.3 %copy-start = (f32[512,512]{1,0:T(8,128)S(1)}, f32[512,512]{1,0:T(8,128)}, u32[]{:S(2)}) copy-start(f32[512,512]{1,0:T(8,128)} %param.25) | copy-start | bytes 3145732
  7.2 27.6 %copy-start.2 = (f32[512,512]{1,0:T(8,128)S(1)}, f32[512,512]{1,0:T(8,128)}, u32[]{:S(2)}) copy-start(f32[512,512]{1,0:T(8,128)} %param.24) | copy-start | bytes 3145732
  8.7 13.8 %all-to-all-start = ((s32[2,2,1,16]{1,0,2,3:T(2,128)}), s32[2,2,1,16]{1,0,2,3:T(2,128)S(1)}, u32[]{:S(2)}, u32[]{:S(2)}) async-start(s32[2,2,1,16]{1,0,2,3:T(2,128)} %copy.22), calls=%async_computation | async-start | bytes 32768 | tf_op jit(solution)/shard_map/all_to_all | solution.py:46
  16.2 22.4 %copy-start.3 = (f32[512,512]{1,0:T(8,128)}, f32[512,512]{1,0:T(8,128)S(1)}, u32[]{:S(2)}) copy-start(f32[512,512]{1,0:T(8,128)S(1)} %fusion.32) | copy-start | bytes 3145732
  22.5 9.9 %all-to-all-start.1 = ((f32[6,2,1,16]{0,1,2,3:T(2,128)}), f32[6,2,1,16]{0,1,2,3:T(2,128)S(1)}, u32[]{:S(2)}, u32[]{:S(2)}) async-start(f32[6,2,1,16]{0,1,2,3:T(2,128)} %copy.24), calls=%async_computation.1 | async-start | bytes 32768 | tf_op jit(solution)/shard_map/all_to_all | solution.py:43
  26.0 115.4 %all-gather.17.cloned.1.call-start = ((), (), s32[]{:S(2)}) async-start(), calls=%async_computation.6 | async-start | bytes 5242880 | tf_op jit(solution)/shard_map/all_gather | solution.py:14
  26.4 11.4 %copy-start.9 = (s32[32]{0:T(128)}, s32[32]{0:T(128)S(1)}, u32[]{:S(2)}) copy-start(s32[32]{0:T(128)S(1)} %eq.62) | copy-start | bytes 388
  33.1 4.7 copy-start.10
  33.5 1.1 copy-start.5
  63.1 155.9 %all-reduce.3.cloned.1.call-start = ((), (), s32[]{:S(2)}) async-start(), calls=%async_computation.2 | async-start | bytes 2097152 | tf_op jit(solution)/shard_map/psum | solution.py:31
  164.0 4.7 copy-start.1
  168.5 132.3 %all-gather.19.cloned.1.call-start = ((), (), s32[]{:S(2)}) async-start(), calls=%async_computation.7 | async-start | bytes 5242880 | tf_op jit(solution)/shard_map/all_gather | solution.py:14
  181.8 153.6 %all-gather.13.cloned.1.call-start = ((), (), s32[]{:S(2)}) async-start(), calls=%async_computation.3 | async-start | bytes 5242880 | tf_op jit(solution)/shard_map/all_gather | solution.py:14
  219.0 251.1 %all-reduce.5.cloned.1.call-start = ((), (), s32[]{:S(2)}) async-start(), calls=%async_computation.4 | async-start | bytes 2097152 | tf_op jit(solution)/shard_map/psum | solution.py:31
  363.1 5.6 %copy-start.8 = (f32[512]{0:T(512)S(1)}, f32[512]{0:T(512)}, u32[]{:S(2)}) copy-start(f32[512]{0:T(512)} %param.27) | copy-start | bytes 6148
  376.0 18.4 %copy-start.6 = (f32[4,512]{1,0:T(4,128)}, f32[4,512]{1,0:T(4,128)S(1)}, u32[]{:S(2)}) copy-start(f32[4,512]{1,0:T(4,128)S(1)} %get-tuple-element.713) | copy-start | bytes 24580
  377.0 17.4 %copy-start.4 = (f32[512,512]{1,0:T(8,128)S(1)}, f32[512,512]{1,0:T(8,128)}, u32[]{:S(2)}) copy-start(f32[512,512]{1,0:T(8,128)} %copy-done.3) | copy-start | bytes 3145732
  419.5 86.1 %all-gather.15.cloned.1.call-start = ((), (), s32[]{:S(2)}) async-start(), calls=%async_computation.5 | async-start | bytes 5242880 | tf_op jit(solution)/shard_map/all_gather | solution.py:14
  522.4 0.6 copy-start.7
Sparse Core Ops, SparseCore 0:
  63.2 78.1 all-gather.16
  168.6 50.3 all-reduce.2
  220.6 80.1 all-gather.18
  302.3 33.0 all-gather.12
  419.6 50.4 all-reduce.4
  471.6 33.9 all-gather.14
where the time goes:
time: 532 us; the launch traced here: 530 us
  waiting for transfers between devices  272 us (51%)
  matrix products  131 us (25%)
  blocking collectives  53.7 us (10%)
  local copies, waits for them, and re-layouts  45.5 us (9%)
  between operations  14.4 us (3%)
  starting transfers between devices  11.3 us (2%)
    all_gather x4, waiting for transfers between devices, entering(): pieces = jax.tree.map(lambda part: lax.all_gather(part, axis), value)  175 us
    dot_general x69, matrix products, product(): jnp.dot(matrix_a, matrix_b, precision=highest, preferred_element_type=jnp...  131 us
    psum x2, waiting for transfers between devices, from_root(): return lax.psum(jnp.where(mine, shard, jnp.zeros_like(shard)), axis)  87.7 us
    all_gather x4, blocking collectives, entering(): pieces = jax.tree.map(lambda part: lax.all_gather(part, axis), value)  34.5 us
    while x16, local copies, waits for them, and re-layouts  22.2 us
    psum x2, blocking collectives, from_root(): return lax.psum(jnp.where(mine, shard, jnp.zeros_like(shard)), axis)  19.2 us
  transfers between devices with their start and end apart: 8, of which 8 were waited for; matrix products, arithmetic and copies ran while one was open for 6% of the time, Pallas kernels for 0%

commit v1 on v0

--- a/solution.py
+++ b/solution.py
@@ -1,6 +1,9 @@
+import functools
 import jax
 import jax.numpy as jnp
 from jax import lax
+from jax.experimental import pallas as pl
+from jax.experimental.pallas import tpu as pltpu
 from jax.sharding import PartitionSpec as P
 
 STEPS_DEV = 4
@@ -136,6 +139,195 @@
     return (filtered, smoothed)
 
 
+bf16 = jnp.bfloat16
+f32 = jnp.float32
+TRANSPOSED = (((1,), (1,)), ((), ()))
+
+
+def split(value):
+    high = value.astype(bf16)
+    return high, (value - high.astype(f32)).astype(bf16)
+
+
+def mul(left, right, dims=(((1,), (0,)), ((), ()))):
+    def one(a, b):
+        return lax.dot_general(a, b, dims, preferred_element_type=f32)
+
+    return one(left[0], right[0]) + (one(left[0], right[1]) + one(left[1], right[0]))
+
+
+def kernel(owners, a_ref, g_ref, s_ref, x0_ref, cols_ref, rows_ref, filt_ref, smooth_ref, bank, small, x_buf, z_buf):
+    states = a_ref.shape[0]
+    slots = rows_ref.shape[1]
+    per_owner = slots // owners
+    tile = 4 * per_owner
+    supers = owners // 4
+    steps = owners * STEPS_DEV
+    span = 4 * STEPS_DEV
+    position = lax.axis_index("tm") * lax.axis_size("ingest") + lax.axis_index("ingest")
+
+    def put(k, value):
+        high, low = split(value)
+        bank[k, 0] = high
+        bank[k, 1] = low
+
+    def get(k):
+        return bank[k, 0], bank[k, 1]
+
+    A, A2, A4, A8, AT, A2T, A4T, A8T, GT, AGT, ST, ST2, ST4, ST8, ST16, ST32, H, PA, RA = range(19)
+    a = a_ref[...]
+    put(A, a)
+    put(AT, a.T)
+    put(GT, g_ref[...].T)
+    put(ST, s_ref[...].T)
+    for src, dst, dst_t in ((A, A2, A2T), (A2, A4, A4T), (A4, A8, A8T)):
+        value = mul(get(src), get(src))
+        put(dst, value)
+        put(dst_t, value.T)
+    put(AGT, mul(get(GT), get(AT)))
+    for src, dst in ((ST, ST2), (ST2, ST4), (ST4, ST8), (ST8, ST16), (ST16, ST32)):
+        put(dst, mul(get(src), get(src)))
+
+    cols = cols_ref[...]
+    step_col = cols[:, 6:7].astype(jnp.int32)
+    used_col = step_col < STEPS_DEV
+    weight_col = jnp.where(used_col, cols[:, 1:2], 0.0)
+    step_col = jnp.where(used_col, step_col, 0)
+    block_col = cols[:, 7:8].astype(jnp.int32)
+    lane = lax.broadcasted_iota(jnp.int32, (slots, states), 1)
+    k = lane & 3
+    pattern = jnp.where(
+        k == 0,
+        cols[:, 2:3],
+        jnp.where(k == 1, cols[:, 3:4], jnp.where(k == 2, cols[:, 4:5], cols[:, 5:6])),
+    )
+    design = jnp.where((lane >> 2) == block_col, pattern, 0.0)
+    put(H, design)
+    put(PA, design)
+    put(RA, mul(get(H), get(AGT)) * weight_col)
+
+    owner_col = lax.broadcasted_iota(jnp.int32, (slots, 1), 0) // per_owner
+    tau_col = (owner_col % 4) * STEPS_DEV + step_col
+    row_values = rows_ref[...]
+    step_row = row_values[6:7].astype(jnp.int32)
+    used_row = step_row < STEPS_DEV
+    weight_row = jnp.where(used_row, row_values[1:2], 0.0)
+    step_row = jnp.where(used_row, step_row, 0)
+    owner_row = lax.broadcasted_iota(jnp.int32, (1, slots), 1) // per_owner
+    tau_row = (owner_row % 4) * STEPS_DEV + step_row
+
+    inverse = [None] * supers
+    for level, (power, power_t) in enumerate(((A, AT), (A2, A2T), (A4, A4T), (A8, A8T))):
+        p, r = get(PA), get(RA)
+        for q in range(supers):
+            part = slice(q * tile, (q + 1) * tile)
+            gram = mul((p[0][part], p[1][part]), (r[0][part], r[1][part]), TRANSPOSED)
+            tc, tr = tau_col[part], tau_row[:, part]
+            keep = ((tc >> (level + 1)) == (tr >> (level + 1))) & (((tc >> level) & 1) == 1)
+            keep = keep & (((tr >> level) & 1) == 0)
+            gram = jnp.where(keep, gram, 0.0)
+            if level == 0:
+                eye = lax.broadcasted_iota(jnp.int32, (tile, tile), 0) == lax.broadcasted_iota(
+                    jnp.int32, (tile, tile), 1
+                )
+                inverse[q] = eye.astype(f32) - gram
+            else:
+                t = split(inverse[q])
+                inverse[q] = inverse[q] - mul(t, split(mul(split(gram), t)))
+        bit_col = ((tau_col >> level) & 1) == 1
+        moved_p = mul(p, get(power))
+        moved_r = mul(r, get(power_t))
+        old_p = p[0].astype(f32) + p[1].astype(f32)
+        old_r = r[0].astype(f32) + r[1].astype(f32)
+        put(PA, jnp.where(bit_col, moved_p, old_p))
+        put(RA, jnp.where(bit_col, old_r, moved_r))
+
+    readings = []
+    p = get(PA)
+    for q in range(supers):
+        part = slice(q * tile, (q + 1) * tile)
+        t = split(inverse[q])
+        seen = mul(t, (p[0][part], p[1][part]))
+        high, low = split(seen.T)
+        small[q, 0] = high
+        small[q, 1] = low
+        y = jnp.broadcast_to(row_values[0:1, part], (16, tile))
+        readings.append(mul(split(y), t, TRANSPOSED))
+
+    state = jnp.broadcast_to(x0_ref[...], (16, states))
+    state = mul(split(state), get(AT))
+    starts, innovations = [], []
+    for q in range(supers):
+        part = slice(q * tile, (q + 1) * tile)
+        starts.append(state)
+        parts = split(state)
+        innovation = readings[q] - mul(parts, (small[q, 0], small[q, 1]))
+        innovations.append(innovation)
+        if q + 1 < supers:
+            half = mul(parts, get(A8T))
+            state = mul(split(half), get(A8T)) + mul(
+                split(innovation), (bank[RA, 0, part], bank[RA, 1, part])
+            )
+    innovation = jnp.concatenate([part[0:1] for part in innovations], axis=1)
+    times = lax.broadcasted_iota(jnp.int32, (steps, 1), 0)
+    here = lax.broadcasted_iota(jnp.int32, (steps, slots), 0) == owner_row * STEPS_DEV + step_row
+    pushes = jnp.where(here, innovation * weight_row, 0.0)
+    pushed = split(mul(split(pushes), get(H)))
+    predicted = pltpu.roll(mul(pushed, get(AGT)), 1, 0)
+    for q in range(supers):
+        predicted = jnp.where(times == q * span, starts[q][0:1], predicted)
+    for level, power_t in enumerate((AT, A2T, A4T, A8T)):
+        reach = 1 << level
+        earlier = jnp.where(times % span >= reach, pltpu.roll(predicted, reach, 0), 0.0)
+        predicted = predicted + mul(split(earlier), get(power_t))
+    filtered = predicted + mul(pushed, get(GT))
+    x_buf[...] = filtered
+    following = jnp.where(times < steps - 1, pltpu.roll(predicted, steps - 1, 0), 0.0)
+    smoothed = filtered - mul(split(following), get(ST))
+    for level, power_t in enumerate((ST, ST2, ST4, ST8, ST16, ST32)):
+        reach = 1 << level
+        later = jnp.where(times < steps - reach, pltpu.roll(smoothed, steps - reach, 0), 0.0)
+        smoothed = smoothed + mul(split(later), get(power_t))
+    z_buf[...] = smoothed
+    base = pl.ds(pl.multiple_of(position // 2 * 8, 8), 8)
+    upper = position % 2 == 1
+    for buf, out_ref in ((x_buf, filt_ref), (z_buf, smooth_ref)):
+        pair = buf[base, :]
+        out_ref[...] = jnp.where(upper, pair[4:8], pair[0:4])
+
+
+def whole_window(transition, gain, smoother_gain, start_state, rows_float, rows_index):
+    states = transition.shape[0]
+    fields = jnp.concatenate([rows_float, rows_index.astype(f32)], axis=0)
+    fields = lax.all_gather(fields, ("tm", "ingest"), axis=2, tiled=True)
+    owners = fields.shape[3]
+    rows = jnp.transpose(fields, (0, 3, 1, 2)).reshape(8, -1)
+    cols = jnp.transpose(rows)
+    slots = rows.shape[1]
+    tile = slots // owners * 4
+    vmem = pl.BlockSpec(memory_space=pltpu.VMEM)
+    return pl.pallas_call(
+        functools.partial(kernel, owners),
+        out_shape=[jax.ShapeDtypeStruct((STEPS_DEV, states), f32)] * 2,
+        in_specs=[vmem] * 6,
+        out_specs=[vmem] * 2,
+        scratch_shapes=[
+            pltpu.VMEM((19, 2, states, states), bf16),
+            pltpu.VMEM((owners // 4, 2, states, tile), bf16),
+            pltpu.VMEM((owners * STEPS_DEV, states), f32),
+            pltpu.VMEM((owners * STEPS_DEV, states), f32),
+        ],
+        compiler_params=pltpu.CompilerParams(vmem_limit_bytes=56 * 1024 * 1024),
+    )(transition, gain, smoother_gain, start_state[None], cols, rows)
+
+
+def on_one(*args):
+    owners = args[4].shape[3]
+    if owners == 16 and args[4].shape[1] * owners == 32:
+        return whole_window(*args)
+    return on_device(*args)
+
+
 def solution(mesh):
     placed = (
         P(),
@@ -146,7 +338,7 @@
         P(None, None, ("groups", "tm", "ingest"), None),
     )
     return jax.shard_map(
-        on_device,
+        on_one,
         mesh=mesh,
         in_specs=placed,
         out_specs=(P(("groups", "tm", "ingest"), None), P(("groups", "tm", "ingest"), None)),

time: 532 us -> 71.4 us (0.13)
  waiting for transfers between devices: 272 us -> 0 us
  matrix products: 131 us -> 0 us
  local copies, waits for them, and re-layouts: 45.5 us -> 1.85 us
  Pallas kernels: 0 us -> 33 us
  blocking collectives: 53.7 us -> 35 us
  between operations: 14.4 us -> 0.63 us
  starting transfers between devices: 11.3 us -> 0 us
    all_gather x4 -> x0, waiting for transfers between devices: 175 us -> none  [entering(): pieces = jax.tree.map(lambda part: lax.all_gather(part, axis), value)]
    dot_general x69 -> x0, matrix products: 131 us -> none  [product(): jnp.dot(matrix_a, matrix_b, precision=highest, preferred_element_type=jnp...]
    psum x2 -> x0, waiting for transfers between devices: 87.7 us -> none  [from_root(): return lax.psum(jnp.where(mine, shard, jnp.zeros_like(shard)), axis)]
    pallas_call x0 -> x1, Pallas kernels: none -> 33 us  [whole_window(): pl.pallas_call(functools.partial(kernel, owners), out_shape=[jax.ShapeDty...]
    while x16 -> x0, local copies, waits for them, and re-layouts: 22.2 us -> none
    psum x2 -> x0, blocking collectives: 19.2 us -> none  [from_root(): return lax.psum(jnp.where(mine, shard, jnp.zeros_like(shard)), axis)]
    all_to_all x2 -> x0, starting transfers between devices: 10.9 us -> none  [the longest x1 7.39 us: on_device(): lax.all_to_all(rows_index, ('tm', 'ingest'), split_axis=3, concat_axis=2,...]
    all_to_all x2 -> x0, waiting for transfers between devices: 9.79 us -> none  [the longest x1 5.95 us: on_device(): lax.all_to_all(rows_float, ('tm', 'ingest'), split_axis=3, concat_axis=2,...]
  transfers between devices with their start and end apart: 8 -> 0, of which waited for: 8 -> 0; matrix products, arithmetic and copies ran while one was open for 6% -> 0% of each run, Pallas kernels for 0% -> 0%
where the time goes in v1:
time: 71.4 us; the launch traced here: 71.2 us
  blocking collectives  35 us (49%)
  Pallas kernels  33 us (46%)
  local copies, waits for them, and re-layouts  1.85 us (3%)
    all_gather x1, blocking collectives, whole_window(): fields = lax.all_gather(fields, ('tm', 'ingest'), axis=2, tiled=True)  35 us
    pallas_call x1, Pallas kernels, whole_window(): pl.pallas_call(functools.partial(kernel, owners), out_shape=[jax.ShapeDty...  33 us

profile of v1, /device:TPU:0, one launch (start us, length us, event | category | flops | bytes accessed | tf_op | source)
XLA Modules:
  0.0 71.2 jit_solution(2422024474232112488)
XLA Ops:
  0.6 0.7 copy_convert_fusion
  1.3 0.7 copy.11
  2.0 35.0 %all_gather.3 = f32[8,2,16,16]{3,0,1,2:T(8,128)S(1)} all-gather(f32[8,2,1,16]{3,0,1,2:T(8,128)S(1)} %pad_maximum_fusion), channel_id=1, replica_groups=mesh['groups'=2,'tm'=4,'ingest'=4] {'tm','ingest'}, dimensions={2}, use_global_device_ids=true | all-gather | bytes 17408 | tf_op jit(solution)/shard_map/all_gather | solution.py:302
  37.0 0.1 copy.12
  37.2 0.2 reshape.7.rows_ref
  37.3 0.0 copy-start
  37.3 0.8 %copy.13.cols_ref = f32[512,8]{1,0:T(8,128)} copy(f32[512,8]{0,1:T(8,128)S(1)} %bitcast.4) | data formatting | bytes 32768 | tf_op jit(solution)/shard_map/transpose | solution.py:305
  38.2 0.0 copy-done
  38.2 33.0 %shard_map.77 = (f32[4,512]{1,0:T(4,128)}, f32[4,512]{1,0:T(4,128)}) custom-call(f32[512,512]{1,0:T(8,128)} %a_ref.1, f32[512,512]{1,0:T(8,128)} %g_ref.1, f32[512,512]{1,0:T(8,128)} %s_ref.1, f32[1,512]{1,0:T(1,128)} %bitcast.5, f32[512,8]{1,0:T(8,128)} %copy.13.cols_ref, f32[8,512]{1,0:T(8,128)} %copy-done), custom_call_target="tpu_custom_call" | custom-call | tf_op jit(solution)/shard_map/pallas_call | solution.py:309
  (1 shorter events, 0.0 us)
Async XLA Ops:
  37.3 0.8 %copy-start = (f32[8,512]{1,0:T(8,128)}, f32[8,512]{1,0:T(8,128)S(1)}, u32[]{:S(2)}) copy-start(f32[8,512]{1,0:T(8,128)S(1)} %reshape.7.rows_ref) | copy-start | bytes 49156

commit v2 on v1

--- a/solution.py
+++ b/solution.py
@@ -153,12 +153,37 @@
     def one(a, b):
         return lax.dot_general(a, b, dims, preferred_element_type=f32)
 
+    count = left[0].shape[0]
+    if count <= 64:
+        both = one(jnp.concatenate(left, axis=0), right[0])
+        return both[:count] + both[count:] + one(left[0], right[1])
     return one(left[0], right[0]) + (one(left[0], right[1]) + one(left[1], right[0]))
 
 
-def kernel(owners, a_ref, g_ref, s_ref, x0_ref, cols_ref, rows_ref, filt_ref, smooth_ref, bank, small, x_buf, z_buf):
-    states = a_ref.shape[0]
-    slots = rows_ref.shape[1]
+def kernel(
+    owners,
+    a_hbm,
+    g_hbm,
+    s_hbm,
+    x0_ref,
+    float_ref,
+    index_ref,
+    filt_ref,
+    smooth_ref,
+    params,
+    bank,
+    small,
+    x_buf,
+    z_buf,
+    sending,
+    arriving,
+    load_sem,
+    send_sem,
+    recv_sem,
+):
+    states = a_hbm.shape[0]
+    cap = float_ref.shape[1]
+    slots = owners * owners * cap
     per_owner = slots // owners
     tile = 4 * per_owner
     supers = owners // 4
@@ -175,20 +200,85 @@
         return bank[k, 0], bank[k, 1]
 
     A, A2, A4, A8, AT, A2T, A4T, A8T, GT, AGT, ST, ST2, ST4, ST8, ST16, ST32, H, PA, RA = range(19)
-    a = a_ref[...]
-    put(A, a)
-    put(AT, a.T)
-    put(GT, g_ref[...].T)
-    put(ST, s_ref[...].T)
+    loads = [
+        pltpu.make_async_copy(hbm, params.at[k], load_sem.at[k])
+        for k, hbm in enumerate((a_hbm, s_hbm, g_hbm))
+    ]
+    for load in loads:
+        load.start()
+    group = lax.axis_index("groups")
+    inner = lax.axis_size("ingest")
+    peers = []
+    for distance in range(1, owners):
+        other = lax.rem(position + distance, owners)
+        peers.append((group, other // inner, lax.rem(other, inner)))
+    barrier = pltpu.get_barrier_semaphore()
+    for peer in peers:
+        pl.semaphore_signal(barrier, inc=1, device_id=peer, device_id_type=pl.DeviceIdType.MESH)
+
+    fields = [
+        jnp.concatenate([float_ref[f, c] for c in range(cap)], axis=1) for f in range(6)
+    ] + [
+        jnp.concatenate([index_ref[f, c] for c in range(cap)], axis=1).astype(f32)
+        for f in range(2)
+    ]
+    own = jnp.concatenate(fields, axis=0)
+    own = jnp.concatenate([own] * 4, axis=1)
+    quarter = lax.broadcasted_iota(jnp.int32, own.shape, 1) // per_owner
+    own = jnp.where(quarter == position % 4, own, 0.0)
+    sending[...] = own
+    arriving[position] = own
+    pl.semaphore_wait(barrier, owners - 1)
+    copies = [
+        pltpu.make_async_remote_copy(
+            src_ref=sending,
+            dst_ref=arriving.at[position],
+            send_sem=send_sem.at[k],
+            recv_sem=recv_sem.at[k],
+            device_id=peer,
+            device_id_type=pl.DeviceIdType.MESH,
+        )
+        for k, peer in enumerate(peers)
+    ]
+    for copy in copies:
+        copy.start()
+
+    loads[0].wait()
+    put(A, params[0])
+    put(AT, params[0].T)
     for src, dst, dst_t in ((A, A2, A2T), (A2, A4, A4T), (A4, A8, A8T)):
         value = mul(get(src), get(src))
         put(dst, value)
         put(dst_t, value.T)
+    loads[1].wait()
+    put(ST, params[1].T)
+    loads[2].wait()
+    put(GT, params[2].T)
     put(AGT, mul(get(GT), get(AT)))
     for src, dst in ((ST, ST2), (ST2, ST4), (ST4, ST8), (ST8, ST16), (ST16, ST32)):
         put(dst, mul(get(src), get(src)))
 
-    cols = cols_ref[...]
+    for copy in copies:
+        copy.wait()
+    quads = []
+    for q in range(owners // 4):
+        quads.append(
+            (arriving[4 * q] + arriving[4 * q + 1]) + (arriving[4 * q + 2] + arriving[4 * q + 3])
+        )
+    mixed = jnp.concatenate(quads, axis=1)
+    from_lane = lax.broadcasted_iota(jnp.int32, (slots, slots), 0)
+    to_lane = lax.broadcasted_iota(jnp.int32, (slots, slots), 1)
+    wanted = (to_lane % per_owner) * owners + to_lane // per_owner
+    order = (from_lane == wanted).astype(bf16)
+    high, low = split(mixed)
+    lowest = (mixed - high.astype(f32) - low.astype(f32)).astype(bf16)
+    ordered = jnp.dot(
+        jnp.concatenate([high, low, lowest, jnp.zeros_like(high)], axis=0),
+        order,
+        preferred_element_type=f32,
+    )
+    row_values = (ordered[0:8] + ordered[8:16]) + ordered[16:24]
+    cols = row_values.T
     step_col = cols[:, 6:7].astype(jnp.int32)
     used_col = step_col < STEPS_DEV
     weight_col = jnp.where(used_col, cols[:, 1:2], 0.0)
@@ -208,7 +298,6 @@
 
     owner_col = lax.broadcasted_iota(jnp.int32, (slots, 1), 0) // per_owner
     tau_col = (owner_col % 4) * STEPS_DEV + step_col
-    row_values = rows_ref[...]
     step_row = row_values[6:7].astype(jnp.int32)
     used_row = step_row < STEPS_DEV
     weight_row = jnp.where(used_row, row_values[1:2], 0.0)
@@ -234,6 +323,23 @@
             else:
                 t = split(inverse[q])
                 inverse[q] = inverse[q] - mul(t, split(mul(split(gram), t)))
+        if level >= 2:
+            run = per_owner << (level - 2)
+
+            def pieces(bit):
+                return [slice(k * run, (k + 1) * run) for k in range(bit, slots // run, 2)]
+
+            for buf, matrix, bit in ((PA, power, 1), (RA, power_t, 0)):
+                chosen = pieces(bit)
+                moving = [
+                    jnp.concatenate([bank[buf, k, part] for part in chosen], axis=0)
+                    for k in range(2)
+                ]
+                high, low = split(mul(moving, get(matrix)))
+                for k, part in enumerate(chosen):
+                    bank[buf, 0, part] = high[k * run : (k + 1) * run]
+                    bank[buf, 1, part] = low[k * run : (k + 1) * run]
+            continue
         bit_col = ((tau_col >> level) & 1) == 1
         moved_p = mul(p, get(power))
         moved_r = mul(r, get(power_t))
@@ -298,27 +404,31 @@
 
 def whole_window(transition, gain, smoother_gain, start_state, rows_float, rows_index):
     states = transition.shape[0]
-    fields = jnp.concatenate([rows_float, rows_index.astype(f32)], axis=0)
-    fields = lax.all_gather(fields, ("tm", "ingest"), axis=2, tiled=True)
-    owners = fields.shape[3]
-    rows = jnp.transpose(fields, (0, 3, 1, 2)).reshape(8, -1)
-    cols = jnp.transpose(rows)
-    slots = rows.shape[1]
-    tile = slots // owners * 4
+    cap, _, owners = rows_float.shape[1:]
+    per_owner = cap * owners
     vmem = pl.BlockSpec(memory_space=pltpu.VMEM)
+    anywhere = pl.BlockSpec(memory_space=pl.ANY)
     return pl.pallas_call(
         functools.partial(kernel, owners),
         out_shape=[jax.ShapeDtypeStruct((STEPS_DEV, states), f32)] * 2,
-        in_specs=[vmem] * 6,
+        in_specs=[anywhere] * 3 + [vmem] * 3,
         out_specs=[vmem] * 2,
         scratch_shapes=[
+            pltpu.VMEM((3, states, states), f32),
             pltpu.VMEM((19, 2, states, states), bf16),
-            pltpu.VMEM((owners // 4, 2, states, tile), bf16),
+            pltpu.VMEM((owners // 4, 2, states, 4 * per_owner), bf16),
             pltpu.VMEM((owners * STEPS_DEV, states), f32),
             pltpu.VMEM((owners * STEPS_DEV, states), f32),
+            pltpu.VMEM((8, 4 * per_owner), f32),
+            pltpu.VMEM((owners, 8, 4 * per_owner), f32),
+            pltpu.SemaphoreType.DMA((3,)),
+            pltpu.SemaphoreType.DMA((owners - 1,)),
+            pltpu.SemaphoreType.DMA((owners - 1,)),
         ],
-        compiler_params=pltpu.CompilerParams(vmem_limit_bytes=56 * 1024 * 1024),
-    )(transition, gain, smoother_gain, start_state[None], cols, rows)
+        compiler_params=pltpu.CompilerParams(
+            vmem_limit_bytes=56 * 1024 * 1024, collective_id=0, has_side_effects=True
+        ),
+    )(transition, gain, smoother_gain, start_state[None], rows_float, rows_index)
 
 
 def on_one(*args):

time: 71.4 us -> 39.2 us (0.55)
  blocking collectives: 35 us -> 0 us
  Pallas kernels: 33 us -> 36.4 us
    all_gather x1 -> x0, blocking collectives: 35 us -> none  [whole_window(): fields = lax.all_gather(fields, ('tm', 'ingest'), axis=2, tiled=True)]
    pallas_call x1, Pallas kernels: 33 us -> 36.4 us  [whole_window(): pl.pallas_call(functools.partial(kernel, owners), out_shape=[jax.ShapeDty...]
    unnamed x3 -> x4, local copies, waits for them, and re-layouts: 0.7 us -> 1.9 us
    transpose x2 -> x0, local copies, waits for them, and re-layouts: 0.96 us -> none  [the longest x1 0.83 us: whole_window(): cols = jnp.transpose(rows)]
where the time goes in v2:
time: 39.2 us; the launch traced here: 39 us
  Pallas kernels  36.4 us (93%)
  local copies, waits for them, and re-layouts  1.9 us (5%)
  between operations  0.65 us (2%)
    pallas_call x1, Pallas kernels, whole_window(): pl.pallas_call(functools.partial(kernel, owners), out_shape=[jax.ShapeDty...  36.4 us
    unnamed x4, local copies, waits for them, and re-layouts  1.9 us

profile of v2, /device:TPU:0, one launch (start us, length us, event | category | flops | bytes accessed | tf_op | source)
XLA Modules:
  0.0 39.0 jit_solution(10431327245673652783)
XLA Ops:
  0.6 36.4 %shard_map.77 = (f32[4,512]{1,0:T(4,128)}, f32[4,512]{1,0:T(4,128)}) custom-call(f32[512,512]{1,0:T(8,128)} %a_hbm.1, f32[512,512]{1,0:T(8,128)} %g_hbm.1, f32[512,512]{1,0:T(8,128)} %s_hbm.1, f32[1,512]{1,0:T(1,128)} %bitcast.1, f32[6,2,1,16]{3,2,1,0:T(1,128)} %float_ref.1, s32[2,2,1,16]{3,2,1,0:T(1,128)} %index_ref.1), custom_call_target="tpu_custom_call" | custom-call | tf_op jit(solution)/shard_map/pallas_call | solution.py:411
  37.1 0.0 copy-start
  37.1 1.3 %copy.10 = f32[4,512]{1,0:T(4,128)} copy(f32[4,512]{1,0:T(4,128)} %get-tuple-element.4) | data formatting | bytes 16384
  38.4 0.0 copy-done
  38.4 0.6 %copy.11 = f32[4,512]{1,0:T(4,128)} copy(f32[4,512]{1,0:T(4,128)S(1)} %copy-done) | data formatting | bytes 16384
Async XLA Ops:
  37.1 1.3 %copy-start = (f32[4,512]{1,0:T(4,128)S(1)}, f32[4,512]{1,0:T(4,128)}, u32[]{:S(2)}) copy-start(f32[4,512]{1,0:T(4,128)} %get-tuple-element.5) | copy-start | bytes 24580

commit v3 on v2

--- a/solution.py
+++ b/solution.py
@@ -168,8 +168,7 @@
     x0_ref,
     float_ref,
     index_ref,
-    filt_ref,
-    smooth_ref,
+    out_ref,
     params,
     bank,
     small,
@@ -228,6 +227,16 @@
     own = jnp.where(quarter == position % 4, own, 0.0)
     sending[...] = own
     arriving[position] = own
+    loads[0].wait()
+    put(A, params[0])
+    put(AT, params[0].T)
+    for src, dst, dst_t in ((A, A2, A2T), (A2, A4, A4T), (A4, A8, A8T)):
+        value = mul(get(src), get(src))
+        put(dst, value)
+        put(dst_t, value.T)
+    loads[2].wait()
+    put(GT, params[2].T)
+    put(AGT, mul(get(GT), get(AT)))
     pl.semaphore_wait(barrier, owners - 1)
     copies = [
         pltpu.make_async_remote_copy(
@@ -243,18 +252,8 @@
     for copy in copies:
         copy.start()
 
-    loads[0].wait()
-    put(A, params[0])
-    put(AT, params[0].T)
-    for src, dst, dst_t in ((A, A2, A2T), (A2, A4, A4T), (A4, A8, A8T)):
-        value = mul(get(src), get(src))
-        put(dst, value)
-        put(dst_t, value.T)
     loads[1].wait()
     put(ST, params[1].T)
-    loads[2].wait()
-    put(GT, params[2].T)
-    put(AGT, mul(get(GT), get(AT)))
     for src, dst in ((ST, ST2), (ST2, ST4), (ST4, ST8), (ST8, ST16), (ST16, ST32)):
         put(dst, mul(get(src), get(src)))
 
@@ -297,68 +296,67 @@
     put(RA, mul(get(H), get(AGT)) * weight_col)
 
     owner_col = lax.broadcasted_iota(jnp.int32, (slots, 1), 0) // per_owner
-    tau_col = (owner_col % 4) * STEPS_DEV + step_col
+    tau_col = owner_col * STEPS_DEV + step_col
     step_row = row_values[6:7].astype(jnp.int32)
     used_row = step_row < STEPS_DEV
     weight_row = jnp.where(used_row, row_values[1:2], 0.0)
     step_row = jnp.where(used_row, step_row, 0)
     owner_row = lax.broadcasted_iota(jnp.int32, (1, slots), 1) // per_owner
-    tau_row = (owner_row % 4) * STEPS_DEV + step_row
-
-    inverse = [None] * supers
+    tau_row = owner_row * STEPS_DEV + step_row
+
+    expected = [
+        jnp.broadcast_to(cols[k : k + 2 * tile, 0:1], (2 * tile, 128))
+        for k in range(0, slots, 2 * tile)
+    ]
     for level, (power, power_t) in enumerate(((A, AT), (A2, A2T), (A4, A4T), (A8, A8T))):
         p, r = get(PA), get(RA)
-        for q in range(supers):
-            part = slice(q * tile, (q + 1) * tile)
-            gram = mul((p[0][part], p[1][part]), (r[0][part], r[1][part]), TRANSPOSED)
+        run = per_owner << max(level - 2, 0)
+        chosen = [slice(k * run, (k + 1) * run) for k in range(slots // run)]
+        later_runs, earlier_runs = chosen[1::2], chosen[0::2]
+        corrections = []
+        for pair in range(supers // 2):
+            part = slice(pair * 2 * tile, (pair + 1) * 2 * tile)
+            p_pair = (p[0][part], p[1][part])
+            gram = mul(p_pair, (r[0][part], r[1][part]), TRANSPOSED)
             tc, tr = tau_col[part], tau_row[:, part]
             keep = ((tc >> (level + 1)) == (tr >> (level + 1))) & (((tc >> level) & 1) == 1)
             keep = keep & (((tr >> level) & 1) == 0)
             gram = jnp.where(keep, gram, 0.0)
-            if level == 0:
-                eye = lax.broadcasted_iota(jnp.int32, (tile, tile), 0) == lax.broadcasted_iota(
-                    jnp.int32, (tile, tile), 1
-                )
-                inverse[q] = eye.astype(f32) - gram
-            else:
-                t = split(inverse[q])
-                inverse[q] = inverse[q] - mul(t, split(mul(split(gram), t)))
+            links = split(gram)
+            expected[pair] = expected[pair] - mul(links, split(expected[pair]))
+            if level >= 2:
+                local = [slice(k * run, (k + 1) * run) for k in range(1, 2 * tile // run, 2)]
+                links = [jnp.concatenate([link[rows] for rows in local], axis=0) for link in links]
+            corrections.append(mul(links, p_pair))
+        correction = jnp.concatenate(corrections, axis=0)
         if level >= 2:
-            run = per_owner << (level - 2)
-
-            def pieces(bit):
-                return [slice(k * run, (k + 1) * run) for k in range(bit, slots // run, 2)]
-
-            for buf, matrix, bit in ((PA, power, 1), (RA, power_t, 0)):
-                chosen = pieces(bit)
+            for buf, matrix, runs in ((PA, power, later_runs), (RA, power_t, earlier_runs)):
                 moving = [
-                    jnp.concatenate([bank[buf, k, part] for part in chosen], axis=0)
-                    for k in range(2)
+                    jnp.concatenate([bank[buf, k, rows] for rows in runs], axis=0) for k in range(2)
                 ]
-                high, low = split(mul(moving, get(matrix)))
-                for k, part in enumerate(chosen):
-                    bank[buf, 0, part] = high[k * run : (k + 1) * run]
-                    bank[buf, 1, part] = low[k * run : (k + 1) * run]
+                moved = mul(moving, get(matrix))
+                if buf == PA:
+                    moved = moved - correction
+                high, low = split(moved)
+                for k, rows in enumerate(runs):
+                    bank[buf, 0, rows] = high[k * run : (k + 1) * run]
+                    bank[buf, 1, rows] = low[k * run : (k + 1) * run]
             continue
         bit_col = ((tau_col >> level) & 1) == 1
         moved_p = mul(p, get(power))
         moved_r = mul(r, get(power_t))
         old_p = p[0].astype(f32) + p[1].astype(f32)
         old_r = r[0].astype(f32) + r[1].astype(f32)
-        put(PA, jnp.where(bit_col, moved_p, old_p))
+        put(PA, jnp.where(bit_col, moved_p, old_p) - correction)
         put(RA, jnp.where(bit_col, old_r, moved_r))
 
     readings = []
-    p = get(PA)
+    expected_row = jnp.concatenate([part.T[0:16] for part in expected], axis=1)
     for q in range(supers):
         part = slice(q * tile, (q + 1) * tile)
-        t = split(inverse[q])
-        seen = mul(t, (p[0][part], p[1][part]))
-        high, low = split(seen.T)
-        small[q, 0] = high
-        small[q, 1] = low
-        y = jnp.broadcast_to(row_values[0:1, part], (16, tile))
-        readings.append(mul(split(y), t, TRANSPOSED))
+        for k in range(2):
+            small[q, k] = bank[PA, k, part].T
+        readings.append(expected_row[:, part])
 
     state = jnp.broadcast_to(x0_ref[...], (16, states))
     state = mul(split(state), get(AT))
@@ -397,9 +395,9 @@
     z_buf[...] = smoothed
     base = pl.ds(pl.multiple_of(position // 2 * 8, 8), 8)
     upper = position % 2 == 1
-    for buf, out_ref in ((x_buf, filt_ref), (z_buf, smooth_ref)):
+    for k, buf in enumerate((x_buf, z_buf)):
         pair = buf[base, :]
-        out_ref[...] = jnp.where(upper, pair[4:8], pair[0:4])
+        out_ref[k * STEPS_DEV : (k + 1) * STEPS_DEV] = jnp.where(upper, pair[4:8], pair[0:4])
 
 
 def whole_window(transition, gain, smoother_gain, start_state, rows_float, rows_index):
@@ -408,11 +406,11 @@
     per_owner = cap * owners
     vmem = pl.BlockSpec(memory_space=pltpu.VMEM)
     anywhere = pl.BlockSpec(memory_space=pl.ANY)
-    return pl.pallas_call(
+    both = pl.pallas_call(
         functools.partial(kernel, owners),
-        out_shape=[jax.ShapeDtypeStruct((STEPS_DEV, states), f32)] * 2,
+        out_shape=jax.ShapeDtypeStruct((2 * STEPS_DEV, states), f32),
         in_specs=[anywhere] * 3 + [vmem] * 3,
-        out_specs=[vmem] * 2,
+        out_specs=vmem,
         scratch_shapes=[
             pltpu.VMEM((3, states, states), f32),
             pltpu.VMEM((19, 2, states, states), bf16),
@@ -429,6 +427,7 @@
             vmem_limit_bytes=56 * 1024 * 1024, collective_id=0, has_side_effects=True
         ),
     )(transition, gain, smoother_gain, start_state[None], rows_float, rows_index)
+    return both[:STEPS_DEV], both[STEPS_DEV:]
 
 
 def on_one(*args):

time: 39.2 us -> 35 us (0.89)
  Pallas kernels: 36.4 us -> 32.7 us
  local copies, waits for them, and re-layouts: 1.9 us -> 1.4 us
    pallas_call x1, Pallas kernels: 36.4 us -> 32.7 us  [whole_window(): pl.pallas_call(functools.partial(kernel, owners), out_shape=jax.ShapeDtyp...]
    unnamed x4 -> x0, local copies, waits for them, and re-layouts: 1.9 us -> none
    slice x0 -> x1, local copies, waits for them, and re-layouts: none -> 1.4 us  [whole_window(): return (both[:STEPS_DEV], both[STEPS_DEV:])]
where the time goes in v3:
time: 35 us; the launch traced here: 34.8 us
  Pallas kernels  32.7 us (93%)
  local copies, waits for them, and re-layouts  1.4 us (4%)
  between operations  0.64 us (2%)
    pallas_call x1, Pallas kernels, whole_window(): pl.pallas_call(functools.partial(kernel, owners), out_shape=jax.ShapeDtyp...  32.7 us
    slice x1, local copies, waits for them, and re-layouts, whole_window(): return (both[:STEPS_DEV], both[STEPS_DEV:])  1.4 us

profile of v3, /device:TPU:0, one launch (start us, length us, event | category | flops | bytes accessed | tf_op | source)
XLA Modules:
  0.0 34.8 jit_solution(17537811255032785508)
XLA Ops:
  0.6 32.7 %shard_map.77 = f32[8,512]{1,0:T(8,128)} custom-call(f32[512,512]{1,0:T(8,128)} %a_hbm.1, f32[512,512]{1,0:T(8,128)} %g_hbm.1, f32[512,512]{1,0:T(8,128)} %s_hbm.1, f32[1,512]{1,0:T(1,128)} %bitcast.1, f32[6,2,1,16]{3,2,1,0:T(1,128)} %float_ref.1, s32[2,2,1,16]{3,2,1,0:T(1,128)} %index_ref.1), custom_call_target="tpu_custom_call" | custom-call | tf_op jit(solution)/shard_map/pallas_call | solution.py:409
  33.4 1.4 %fusion = (f32[4,512]{1,0:T(4,128)}, f32[4,512]{1,0:T(4,128)}) fusion(f32[8,512]{1,0:T(8,128)} %shard_map.77), kind=kLoop, calls=%fused_computation | loop fusion | bytes 32768 | tf_op jit(solution)/shard_map/slice | solution.py:430

commit v4 on v3

--- a/solution.py
+++ b/solution.py
@@ -198,7 +198,7 @@
     def get(k):
         return bank[k, 0], bank[k, 1]
 
-    A, A2, A4, A8, AT, A2T, A4T, A8T, GT, AGT, ST, ST2, ST4, ST8, ST16, ST32, H, PA, RA = range(19)
+    A, A2, A4, A8, AT, A2T, A4T, A8T, GT, AGT, ST, ST2, ST4, ST8, H, PA, RA = range(17)
     loads = [
         pltpu.make_async_copy(hbm, params.at[k], load_sem.at[k])
         for k, hbm in enumerate((a_hbm, s_hbm, g_hbm))
@@ -234,9 +234,6 @@
         value = mul(get(src), get(src))
         put(dst, value)
         put(dst_t, value.T)
-    loads[2].wait()
-    put(GT, params[2].T)
-    put(AGT, mul(get(GT), get(AT)))
     pl.semaphore_wait(barrier, owners - 1)
     copies = [
         pltpu.make_async_remote_copy(
@@ -252,9 +249,12 @@
     for copy in copies:
         copy.start()
 
+    loads[2].wait()
+    put(GT, params[2].T)
+    put(AGT, mul(get(GT), get(AT)))
     loads[1].wait()
     put(ST, params[1].T)
-    for src, dst in ((ST, ST2), (ST2, ST4), (ST4, ST8), (ST8, ST16), (ST16, ST32)):
+    for src, dst in ((ST, ST2), (ST2, ST4), (ST4, ST8)):
         put(dst, mul(get(src), get(src)))
 
     for copy in copies:
@@ -388,11 +388,16 @@
     x_buf[...] = filtered
     following = jnp.where(times < steps - 1, pltpu.roll(predicted, steps - 1, 0), 0.0)
     smoothed = filtered - mul(split(following), get(ST))
-    for level, power_t in enumerate((ST, ST2, ST4, ST8, ST16, ST32)):
+    for level, power_t in enumerate((ST, ST2, ST4)):
         reach = 1 << level
         later = jnp.where(times < steps - reach, pltpu.roll(smoothed, steps - reach, 0), 0.0)
         smoothed = smoothed + mul(split(later), get(power_t))
     z_buf[...] = smoothed
+    entering_rows = smoothed[steps - 8 :]
+    for row in range(steps - 16, -8, -8):
+        twice = jnp.concatenate([entering_rows, entering_rows], axis=0)
+        entering_rows = smoothed[row : row + 8] + mul(split(twice), get(ST8))[0:8]
+        z_buf[row : row + 8, :] = entering_rows
     base = pl.ds(pl.multiple_of(position // 2 * 8, 8), 8)
     upper = position % 2 == 1
     for k, buf in enumerate((x_buf, z_buf)):
@@ -413,7 +418,7 @@
         out_specs=vmem,
         scratch_shapes=[
             pltpu.VMEM((3, states, states), f32),
-            pltpu.VMEM((19, 2, states, states), bf16),
+            pltpu.VMEM((17, 2, states, states), bf16),
             pltpu.VMEM((owners // 4, 2, states, 4 * per_owner), bf16),
             pltpu.VMEM((owners * STEPS_DEV, states), f32),
             pltpu.VMEM((owners * STEPS_DEV, states), f32),

time: 35 us -> 34.9 us (level)
  no operation moved by 1% of the time
where the time goes in v4:
time: 34.9 us; the launch traced here: 34.6 us
  Pallas kernels  32.5 us (93%)
  local copies, waits for them, and re-layouts  1.4 us (4%)
  between operations  0.64 us (2%)
    pallas_call x1, Pallas kernels, whole_window(): pl.pallas_call(functools.partial(kernel, owners), out_shape=jax.ShapeDtyp...  32.5 us
    slice x1, local copies, waits for them, and re-layouts, whole_window(): return (both[:STEPS_DEV], both[STEPS_DEV:])  1.4 us

profile of v4, /device:TPU:0, one launch (start us, length us, event | category | flops | bytes accessed | tf_op | source)
XLA Modules:
  0.0 34.6 jit_solution(8270514376355632028)
XLA Ops:
  0.6 32.5 %shard_map.77 = f32[8,512]{1,0:T(8,128)} custom-call(f32[512,512]{1,0:T(8,128)} %a_hbm.1, f32[512,512]{1,0:T(8,128)} %g_hbm.1, f32[512,512]{1,0:T(8,128)} %s_hbm.1, f32[1,512]{1,0:T(1,128)} %bitcast.1, f32[6,2,1,16]{3,2,1,0:T(1,128)} %float_ref.1, s32[2,2,1,16]{3,2,1,0:T(1,128)} %index_ref.1), custom_call_target="tpu_custom_call" | custom-call | tf_op jit(solution)/shard_map/pallas_call | solution.py:414
  33.2 1.4 %fusion = (f32[4,512]{1,0:T(4,128)}, f32[4,512]{1,0:T(4,128)}) fusion(f32[8,512]{1,0:T(8,128)} %shard_map.77), kind=kLoop, calls=%fused_computation | loop fusion | bytes 32768 | tf_op jit(solution)/shard_map/slice | solution.py:435
